TPU v7x, 32 devices: a whole 2x2x4 slice. The times are simulated.
32 devices in a mesh: seg: 4 (over y, core), pan: 8 (over z, x).
Axes of the slice: x: 2, y: 2, z: 4, core: 2. Of those that a mesh axis runs over, the one named last changes fastest.
Arguments:
- sources: bfloat16 [2, 2, 64, 65536], P(None, None, 'seg', 'pan'), may hold values from -3 to 3
- panel_geom: float32 [6, 65536], P(None, 'pan'), may hold values from -1 to 1, as said below
- mic_pos: float32 [3, 1024], replicated, may hold values from -12 to 12, as said below
- mic_order: int32 [1024], replicated, may hold values from 0 to 1023, each once
Outputs:
- csm: float32 [2, 1024, 1024], P(None, 'pan', 'seg')
Inputs may be any that keep to these rules, and one draw needn't show every extreme that they name: `mic_order`: each of the 1024 microphones stands exactly once. `panel_geom`: panel centres lie on a cylinder of radius 1 around the first axis with first coordinate within -1 to 1; normals are the unit radial directions. `mic_pos`: microphones lie at distances 6 to 12 from the anchor (0, 0, 0).
All inputs are finite; a program needn't handle non-finite values.
Results may differ from a plain program's by a relative error of at most 0.0039.
Values may be sent and summed in bfloat16 or wider, within the bound.
A program may use at most 64 MiB of HBM per device.

v0:
```python
import math

import jax
import jax.numpy as jnp
from jax import lax
from jax.sharding import PartitionSpec as P

mach_number = 0.3
beta_sq = 0.91
wave_number = 40.0


def kernel_block(mics, geometry):
    dx = mics[0][:, None] - geometry[0][None, :]
    dy = mics[1][:, None] - geometry[1][None, :]
    dz = mics[2][:, None] - geometry[2][None, :]
    rstar = jnp.sqrt(dx * dx + beta_sq * (dy * dy + dz * dz))
    radius = (rstar - mach_number * dx) / beta_sq
    phase = wave_number * radius
    amplitude = 1.0 / (4.0 * math.pi * rstar)
    green_re = amplitude * jnp.cos(phase)
    green_im = -amplitude * jnp.sin(phase)
    normal_part = (
        dx * geometry[3][None, :] + dy * geometry[4][None, :] + dz * geometry[5][None, :]
    ) / rstar
    scale_re = normal_part / (wave_number * rstar)
    dip_re = scale_re * green_re - normal_part * green_im
    dip_im = scale_re * green_im + normal_part * green_re
    return jnp.concatenate([green_re, green_im, dip_re, dip_im], axis=1).astype(jnp.bfloat16)


def block_weights(piece):
    swapped = jnp.transpose(piece, (0, 1, 3, 2))
    real_cols = jnp.concatenate(
        [swapped[0, 0], -swapped[1, 0], swapped[0, 1], -swapped[1, 1]], axis=0
    )
    imag_cols = jnp.concatenate(
        [swapped[1, 0], swapped[0, 0], swapped[1, 1], swapped[0, 1]], axis=0
    )
    return jnp.concatenate([real_cols, imag_cols], axis=1)


def split_sources(sources, blocks, block_size):
    shaped = sources.reshape(2, 2, sources.shape[2], blocks, block_size)
    return jnp.transpose(shaped, (3, 0, 1, 2, 4))


def panel_spectra(mics, geom_blocks, source_blocks):

    def step(running, pair):
        geometry, piece = pair
        weights = block_weights(piece)
        return (
            running
            + jnp.dot(kernel_block(mics, geometry), weights, preferred_element_type=jnp.float32),
            None,
        )

    init = jnp.zeros((mics.shape[1], 2 * source_blocks.shape[3]), jnp.float32)
    summed, unused = lax.scan(step, init, (geom_blocks, source_blocks))
    return summed


def summed_spectra(mic_rows, geom_blocks, source_blocks):
    local_terms = panel_spectra(mic_rows, geom_blocks, source_blocks)
    return lax.psum(local_terms, "pan")


def cross_terms(own_rows, columns):
    half = columns.shape[1] // 2
    rows_re = own_rows[:, :half]
    rows_im = own_rows[:, half:]
    cols_re = columns[:, :half]
    cols_im = columns[:, half:]
    highest = lax.Precision.HIGHEST
    csm_re = jnp.dot(rows_re, cols_re.T, precision=highest) + jnp.dot(
        rows_im, cols_im.T, precision=highest
    )
    csm_im = jnp.dot(rows_im, cols_re.T, precision=highest) - jnp.dot(
        rows_re, cols_im.T, precision=highest
    )
    return jnp.stack([csm_re, csm_im])


def shards(sources, panel_geom, mic_pos, mic_order):
    ordered = jnp.take(mic_pos, mic_order, axis=1)
    panels_here = panel_geom.shape[1]
    block_size = min(512, panels_here)
    blocks = panels_here // block_size
    geom_blocks = jnp.transpose(panel_geom.reshape(6, blocks, block_size), (1, 0, 2))
    mics_all = ordered.shape[1]
    seg_count = lax.axis_size("seg")
    row_count = mics_all // lax.axis_size("pan")
    row_start = lax.axis_index("pan") * row_count
    source_blocks = split_sources(sources, blocks, block_size)
    spectra = summed_spectra(ordered, geom_blocks, source_blocks)
    own_rows = lax.dynamic_slice_in_dim(spectra, row_start, row_count, 0)
    partial_csm = cross_terms(own_rows, spectra)
    summed = lax.psum_scatter(partial_csm, "seg", scatter_dimension=2, tiled=True)
    return summed / (own_rows.shape[1] // 2 * seg_count)


def solution(mesh):
    placed = (P(None, None, "seg", "pan"), P(None, "pan"), P(), P())
    return jax.shard_map(
        shards, mesh=mesh, in_specs=placed, out_specs=P(None, "pan", "seg"), check_vma=False
    )
```

profile of v0, /device:TPU:0, one launch (start us, length us, event | category | flops | bytes accessed | tf_op | source)
XLA Modules:
  0.0 393.6 jit_solution(11039744929572009952)
XLA Ops:
  7.9 1.0 copy.7
  9.0 2.8 gather_fusion
  12.5 1.5 copy.9
  14.1 267.9 %while.13 = (s32[]{:T(128)}, f32[1024,32]{0,1:T(8,128)S(1)}, f32[3,1024]{1,0:T(4,128)S(1)}, f32[16,6,512]{2,1,0:T(8,128)}, bf16[16,2,2,16,512]{4,3,2,1,0:T(8,128...) while((s32[]{:T(128)}, f32[1024,32]{0,1:T(8,128)S(1)}, ...), condition=%wide.region_1.2_spmd.clone, body=%wide.region_0.1_spmd.clone.sunk | while | flops 170999808 | bytes 9150687 | solution.py:60
  15.1 12.3 %subtract_convert_fusion.2 = (bf16[1024,512]{1,0:T(8,128)(2,1)S(1)}, bf16[1024,512]{1,0:T(8,128)(2,1)S(1)}, bf16[1024,512]{1,0:T(8,128)(2,1)S(1)}, bf16[1024,512]{1,0:T(8,128)(2,1)}) fusion(f32[512]{0:T(512)S(1)} %bitcast.75, f32[512]{0:T(512)S(1)} %bitcast.73, f32[1024]{0:T(1024)S(1)} %bitcast.68, f32[512]{0:T(512)S(1)} %bitcast.71, ...), kind=kLoop, calls=%fused_computation.28.clone.1 | loop fusion | flops 18874368 | bytes 4218880 | tf_op jit(solution)/shard_map/convert.2
  28.2 2.6 fusion.66
  31.8 12.3 %subtract_convert_fusion.2 = (bf16[1024,512]{1,0:T(8,128)(2,1)S(1)}, bf16[1024,512]{1,0:T(8,128)(2,1)S(1)}, bf16[1024,512]{1,0:T(8,128)(2,1)S(1)}, bf16[1024,512]{1,0:T(8,128)(2,1)}) fusion(f32[512]{0:T(512)S(1)} %bitcast.75, f32[512]{0:T(512)S(1)} %bitcast.73, f32[1024]{0:T(1024)S(1)} %bitcast.68, f32[512]{0:T(512)S(1)} %bitcast.71, ...), kind=kLoop, calls=%fused_computation.28.clone.1 | loop fusion | flops 18874368 | bytes 4218880 | tf_op jit(solution)/shard_map/convert.2
  45.0 2.6 fusion.66
  47.5 1.0 constant_dynamic-slice_fusion.7
  48.5 12.3 %subtract_convert_fusion.2 = (bf16[1024,512]{1,0:T(8,128)(2,1)S(1)}, bf16[1024,512]{1,0:T(8,128)(2,1)S(1)}, bf16[1024,512]{1,0:T(8,128)(2,1)S(1)}, bf16[1024,512]{1,0:T(8,128)(2,1)}) fusion(f32[512]{0:T(512)S(1)} %bitcast.75, f32[512]{0:T(512)S(1)} %bitcast.73, f32[1024]{0:T(1024)S(1)} %bitcast.68, f32[512]{0:T(512)S(1)} %bitcast.71, ...), kind=kLoop, calls=%fused_computation.28.clone.1 | loop fusion | flops 18874368 | bytes 4218880 | tf_op jit(solution)/shard_map/convert.2
  61.7 2.6 fusion.66
  65.3 12.3 %subtract_convert_fusion.2 = (bf16[1024,512]{1,0:T(8,128)(2,1)S(1)}, bf16[1024,512]{1,0:T(8,128)(2,1)S(1)}, bf16[1024,512]{1,0:T(8,128)(2,1)S(1)}, bf16[1024,512]{1,0:T(8,128)(2,1)}) fusion(f32[512]{0:T(512)S(1)} %bitcast.75, f32[512]{0:T(512)S(1)} %bitcast.73, f32[1024]{0:T(1024)S(1)} %bitcast.68, f32[512]{0:T(512)S(1)} %bitcast.71, ...), kind=kLoop, calls=%fused_computation.28.clone.1 | loop fusion | flops 18874368 | bytes 4218880 | tf_op jit(solution)/shard_map/convert.2
  78.4 2.6 fusion.66
  81.0 1.0 constant_dynamic-slice_fusion.7
  82.0 12.3 %subtract_convert_fusion.2 = (bf16[1024,512]{1,0:T(8,128)(2,1)S(1)}, bf16[1024,512]{1,0:T(8,128)(2,1)S(1)}, bf16[1024,512]{1,0:T(8,128)(2,1)S(1)}, bf16[1024,512]{1,0:T(8,128)(2,1)}) fusion(f32[512]{0:T(512)S(1)} %bitcast.75, f32[512]{0:T(512)S(1)} %bitcast.73, f32[1024]{0:T(1024)S(1)} %bitcast.68, f32[512]{0:T(512)S(1)} %bitcast.71, ...), kind=kLoop, calls=%fused_computation.28.clone.1 | loop fusion | flops 18874368 | bytes 4218880 | tf_op jit(solution)/shard_map/convert.2
  95.2 2.6 fusion.66
  97.8 1.0 constant_dynamic-slice_fusion.7
  98.7 12.3 %subtract_convert_fusion.2 = (bf16[1024,512]{1,0:T(8,128)(2,1)S(1)}, bf16[1024,512]{1,0:T(8,128)(2,1)S(1)}, bf16[1024,512]{1,0:T(8,128)(2,1)S(1)}, bf16[1024,512]{1,0:T(8,128)(2,1)}) fusion(f32[512]{0:T(512)S(1)} %bitcast.75, f32[512]{0:T(512)S(1)} %bitcast.73, f32[1024]{0:T(1024)S(1)} %bitcast.68, f32[512]{0:T(512)S(1)} %bitcast.71, ...), kind=kLoop, calls=%fused_computation.28.clone.1 | loop fusion | flops 18874368 | bytes 4218880 | tf_op jit(solution)/shard_map/convert.2
  111.9 2.6 fusion.66
  114.5 1.0 constant_dynamic-slice_fusion.7
  115.5 12.3 %subtract_convert_fusion.2 = (bf16[1024,512]{1,0:T(8,128)(2,1)S(1)}, bf16[1024,512]{1,0:T(8,128)(2,1)S(1)}, bf16[1024,512]{1,0:T(8,128)(2,1)S(1)}, bf16[1024,512]{1,0:T(8,128)(2,1)}) fusion(f32[512]{0:T(512)S(1)} %bitcast.75, f32[512]{0:T(512)S(1)} %bitcast.73, f32[1024]{0:T(1024)S(1)} %bitcast.68, f32[512]{0:T(512)S(1)} %bitcast.71, ...), kind=kLoop, calls=%fused_computation.28.clone.1 | loop fusion | flops 18874368 | bytes 4218880 | tf_op jit(solution)/shard_map/convert.2
  128.6 2.6 fusion.66
  131.2 1.0 constant_dynamic-slice_fusion.7
  132.2 12.3 %subtract_convert_fusion.2 = (bf16[1024,512]{1,0:T(8,128)(2,1)S(1)}, bf16[1024,512]{1,0:T(8,128)(2,1)S(1)}, bf16[1024,512]{1,0:T(8,128)(2,1)S(1)}, bf16[1024,512]{1,0:T(8,128)(2,1)}) fusion(f32[512]{0:T(512)S(1)} %bitcast.75, f32[512]{0:T(512)S(1)} %bitcast.73, f32[1024]{0:T(1024)S(1)} %bitcast.68, f32[512]{0:T(512)S(1)} %bitcast.71, ...), kind=kLoop, calls=%fused_computation.28.clone.1 | loop fusion | flops 18874368 | bytes 4218880 | tf_op jit(solution)/shard_map/convert.2
  145.4 2.6 fusion.66
  148.9 12.3 %subtract_convert_fusion.2 = (bf16[1024,512]{1,0:T(8,128)(2,1)S(1)}, bf16[1024,512]{1,0:T(8,128)(2,1)S(1)}, bf16[1024,512]{1,0:T(8,128)(2,1)S(1)}, bf16[1024,512]{1,0:T(8,128)(2,1)}) fusion(f32[512]{0:T(512)S(1)} %bitcast.75, f32[512]{0:T(512)S(1)} %bitcast.73, f32[1024]{0:T(1024)S(1)} %bitcast.68, f32[512]{0:T(512)S(1)} %bitcast.71, ...), kind=kLoop, calls=%fused_computation.28.clone.1 | loop fusion | flops 18874368 | bytes 4218880 | tf_op jit(solution)/shard_map/convert.2
  162.1 2.6 fusion.66
  165.7 12.3 %subtract_convert_fusion.2 = (bf16[1024,512]{1,0:T(8,128)(2,1)S(1)}, bf16[1024,512]{1,0:T(8,128)(2,1)S(1)}, bf16[1024,512]{1,0:T(8,128)(2,1)S(1)}, bf16[1024,512]{1,0:T(8,128)(2,1)}) fusion(f32[512]{0:T(512)S(1)} %bitcast.75, f32[512]{0:T(512)S(1)} %bitcast.73, f32[1024]{0:T(1024)S(1)} %bitcast.68, f32[512]{0:T(512)S(1)} %bitcast.71, ...), kind=kLoop, calls=%fused_computation.28.clone.1 | loop fusion | flops 18874368 | bytes 4218880 | tf_op jit(solution)/shard_map/convert.2
  178.8 2.6 fusion.66
  182.4 12.3 %subtract_convert_fusion.2 = (bf16[1024,512]{1,0:T(8,128)(2,1)S(1)}, bf16[1024,512]{1,0:T(8,128)(2,1)S(1)}, bf16[1024,512]{1,0:T(8,128)(2,1)S(1)}, bf16[1024,512]{1,0:T(8,128)(2,1)}) fusion(f32[512]{0:T(512)S(1)} %bitcast.75, f32[512]{0:T(512)S(1)} %bitcast.73, f32[1024]{0:T(1024)S(1)} %bitcast.68, f32[512]{0:T(512)S(1)} %bitcast.71, ...), kind=kLoop, calls=%fused_computation.28.clone.1 | loop fusion | flops 18874368 | bytes 4218880 | tf_op jit(solution)/shard_map/convert.2
  195.6 2.6 fusion.66
  199.2 12.3 %subtract_convert_fusion.2 = (bf16[1024,512]{1,0:T(8,128)(2,1)S(1)}, bf16[1024,512]{1,0:T(8,128)(2,1)S(1)}, bf16[1024,512]{1,0:T(8,128)(2,1)S(1)}, bf16[1024,512]{1,0:T(8,128)(2,1)}) fusion(f32[512]{0:T(512)S(1)} %bitcast.75, f32[512]{0:T(512)S(1)} %bitcast.73, f32[1024]{0:T(1024)S(1)} %bitcast.68, f32[512]{0:T(512)S(1)} %bitcast.71, ...), kind=kLoop, calls=%fused_computation.28.clone.1 | loop fusion | flops 18874368 | bytes 4218880 | tf_op jit(solution)/shard_map/convert.2
  212.3 2.6 fusion.66
  215.9 12.3 %subtract_convert_fusion.2 = (bf16[1024,512]{1,0:T(8,128)(2,1)S(1)}, bf16[1024,512]{1,0:T(8,128)(2,1)S(1)}, bf16[1024,512]{1,0:T(8,128)(2,1)S(1)}, bf16[1024,512]{1,0:T(8,128)(2,1)}) fusion(f32[512]{0:T(512)S(1)} %bitcast.75, f32[512]{0:T(512)S(1)} %bitcast.73, f32[1024]{0:T(1024)S(1)} %bitcast.68, f32[512]{0:T(512)S(1)} %bitcast.71, ...), kind=kLoop, calls=%fused_computation.28.clone.1 | loop fusion | flops 18874368 | bytes 4218880 | tf_op jit(solution)/shard_map/convert.2
  229.1 2.6 fusion.66
  232.6 12.3 %subtract_convert_fusion.2 = (bf16[1024,512]{1,0:T(8,128)(2,1)S(1)}, bf16[1024,512]{1,0:T(8,128)(2,1)S(1)}, bf16[1024,512]{1,0:T(8,128)(2,1)S(1)}, bf16[1024,512]{1,0:T(8,128)(2,1)}) fusion(f32[512]{0:T(512)S(1)} %bitcast.75, f32[512]{0:T(512)S(1)} %bitcast.73, f32[1024]{0:T(1024)S(1)} %bitcast.68, f32[512]{0:T(512)S(1)} %bitcast.71, ...), kind=kLoop, calls=%fused_computation.28.clone.1 | loop fusion | flops 18874368 | bytes 4218880 | tf_op jit(solution)/shard_map/convert.2
  245.8 2.6 fusion.66
  248.4 1.1 constant_dynamic-slice_fusion.7
  249.5 12.3 %subtract_convert_fusion.2 = (bf16[1024,512]{1,0:T(8,128)(2,1)S(1)}, bf16[1024,512]{1,0:T(8,128)(2,1)S(1)}, bf16[1024,512]{1,0:T(8,128)(2,1)S(1)}, bf16[1024,512]{1,0:T(8,128)(2,1)}) fusion(f32[512]{0:T(512)S(1)} %bitcast.75, f32[512]{0:T(512)S(1)} %bitcast.73, f32[1024]{0:T(1024)S(1)} %bitcast.68, f32[512]{0:T(512)S(1)} %bitcast.71, ...), kind=kLoop, calls=%fused_computation.28.clone.1 | loop fusion | flops 18874368 | bytes 4218880 | tf_op jit(solution)/shard_map/convert.2
  262.7 2.6 fusion.66
  266.3 12.3 %subtract_convert_fusion.2 = (bf16[1024,512]{1,0:T(8,128)(2,1)S(1)}, bf16[1024,512]{1,0:T(8,128)(2,1)S(1)}, bf16[1024,512]{1,0:T(8,128)(2,1)S(1)}, bf16[1024,512]{1,0:T(8,128)(2,1)}) fusion(f32[512]{0:T(512)S(1)} %bitcast.75, f32[512]{0:T(512)S(1)} %bitcast.73, f32[1024]{0:T(1024)S(1)} %bitcast.68, f32[512]{0:T(512)S(1)} %bitcast.71, ...), kind=kLoop, calls=%fused_computation.28.clone.1 | loop fusion | flops 18874368 | bytes 4218880 | tf_op jit(solution)/shard_map/convert.2
  279.4 2.6 fusion.66
  282.7 72.5 %all-reduce.2.cloned.1.call-done = f32[1024,32]{0,1:T(8,128)} async-done(((f32[1024,32]{0,1:T(8,128)}), f32[1024,32]{0,1:T(8,128)}) %all-reduce.2.cloned.1.call-update) | async-done | bytes 131088 | tf_op jit(solution)/shard_map/psum | solution.py:66
  355.3 1.6 fusion.47
  356.9 1.5 fusion.45
  359.7 1.1 pad_maximum_fusion
  360.8 24.3 %reduce-scatter.2.cloned.1.call-done = f32[2,128,256]{2,1,0:T(8,128)} async-done(((f32[2,128,1024]{2,1,0:T(8,128)}), f32[2,128,256]{2,1,0:T(8,128)}) %reduce-scatter.2.cloned.1.call-update) | async-done | bytes 262160 | tf_op jit(solution)/shard_map/reduce_scatter | solution.py:99
  385.1 1.7 broadcast_multiply_fusion
  (92 shorter events, 27.7 us)
Async XLA Ops:
  6.5 348.7 %all-reduce.2.cloned.1.call-start = ((), (), s32[]{:S(2)}) async-start(), calls=%async_computation.1 | async-start | bytes 262144 | tf_op jit(solution)/shard_map/psum | solution.py:66
  7.9 4.2 %copy-start = (bf16[2,2,16,8192]{3,2,1,0:T(8,128)(2,1)S(1)}, bf16[2,2,16,8192]{3,2,1,0:T(8,128)(2,1)}, u32[]{:S(2)}) copy-start(bf16[2,2,16,8192]{3,2,1,0:T(8,128)(2,1)} %param.6) | copy-start | bytes 3145732
  282.0 0.7 copy-start.2
  282.7 102.4 %reduce-scatter.2.cloned.1.call-start = ((), (), s32[]{:S(2)}) async-start(), calls=%async_computation.2 | async-start | bytes 1310720 | tf_op jit(solution)/shard_map/reduce_scatter | solution.py:99
  355.3 3.1 copy-start.1
Sparse Core Ops, SparseCore 0:
  282.8 72.4 all-reduce.1
  360.9 24.1 reduce-scatter.1
where the time goes:
time: 396 us; the launch traced here: 394 us
  other arithmetic  201 us (51%)
  waiting for transfers between devices  96.9 us (24%)
  matrix products  45.4 us (11%)
  local copies, waits for them, and re-layouts  35.9 us (9%)
  between operations  13.5 us (3%)
    another operation x16, other arithmetic  197 us
    psum x1, waiting for transfers between devices, summed_spectra(): return lax.psum(local_terms, 'pan')  72.5 us
    dot_general x16, matrix products, step(): jnp.dot(kernel_block(mics, geometry), weights, preferred_element_type=jnp...  41.1 us
    reduce_scatter x1, waiting for transfers between devices, shards(): lax.psum_scatter(partial_csm, 'seg', scatter_dimension=2, tiled=True)  24.3 us
    slice x32, local copies, waits for them, and re-layouts, kernel_block(): dx = mics[0][:, None] - geometry[0][None, :]  15.7 us
    transpose x16, local copies, waits for them, and re-layouts, block_weights(): swapped = jnp.transpose(piece, (0, 1, 3, 2))  13.5 us
  transfers between devices with their start and end apart: 2, of which 2 were waited for; matrix products, arithmetic and copies ran while one was open for 0% of the time, Pallas kernels for 0%

commit v1 on v0

v1 whole, which is shorter than its diff:
```python
import functools
import math

import jax
import jax.numpy as jnp
import numpy as np
from jax import lax
from jax.experimental import pallas as pl
from jax.experimental.pallas import tpu as pltpu
from jax.sharding import PartitionSpec as P

mach_number = 0.3
beta_sq = 0.91
wave_number = 40.0

MESH = pl.DeviceIdType.MESH
LANES = 128
SUB_ROWS = 32
TURN = wave_number / (beta_sq * 2.0 * math.pi)
BETA = math.sqrt(beta_sq)


def fit(function, degree_even, half_range, odd):
    count = degree_even + 1
    nodes = np.cos((np.arange(200) + 0.5) * math.pi / 200)
    u = (nodes + 1) / 2 * half_range**2
    x = np.sqrt(u)
    y = function(x) / x if odd else function(x)
    cheb = np.polynomial.chebyshev.Chebyshev.fit(
        u, y, count - 1, domain=[0, half_range**2]
    )
    return [float(v) for v in cheb.convert(kind=np.polynomial.Polynomial).coef]


ROOT2 = math.sqrt(2.0)
SIN_COEF = fit(lambda x: ROOT2 * np.sin(math.pi * x), 4, 0.5, True)
COS_COEF = fit(lambda x: ROOT2 * np.cos(math.pi * x), 4, 0.5, False)


def horner(coef, u):
    total = coef[-1]
    for c in coef[-2::-1]:
        total = total * u + c
    return total


def pair_terms(mx, my, mz, panel):
    cx, cy, cz, n0, n1, n2 = panel
    dx = mx - cx
    dy = my - cy
    dz = mz - cz
    sq = dx * dx + (dy * dy + dz * dz)
    inv = lax.rsqrt(sq)
    turns = sq * inv - mach_number * dx
    magic = 12582912.0
    whole = (turns + magic) - magic
    f = turns - whole
    u = f * f
    s = horner(SIN_COEF, u) * f
    c = horner(COS_COEF, u)
    amplitude = inv * (TURN / (4.0 * math.pi))
    green_re = amplitude * (1.0 - s * s)
    green_im_neg = amplitude * (s * c)
    normal_part = (dx * n0 + (dy * n1 + dz * n2)) * inv
    near = inv * (TURN / wave_number)
    dip_re = normal_part * (near * green_re + green_im_neg)
    dip_im = normal_part * (green_re - near * green_im_neg)
    return green_re, -green_im_neg, dip_re, dip_im


def kernel(cfg, src, geom, mics, order, out, src_buf, geo, micb, g_buf, r1, r2, spec,
           rs_buf, own, cols, rows, loc_sem, core_sems, y_send, y_recv, f_send, f_recv,
           rs_send, rs_recv, col_send, col_recv, row_send, row_recv):
    n_seg, n_pan, segs_here, half, block, chunk, n_own, rows_per, pieces = cfg
    n_split = n_seg // 2
    n_red = n_split * n_pan
    n_row_chunks = rows_per // chunk
    s = lax.axis_index("seg")
    p = lax.axis_index("pan")
    y = s // 2
    c = lax.rem(s, 2)
    me = y * n_pan + p
    core_peer = (y * 2 + 1 - c, p)
    m_own = s * block + chunk * p
    p_r = m_own // rows_per
    row_slot = (m_own - p_r * rows_per) // chunk
    owner = p < n_own

    def row_owner(k):
        m = rows_per * p + chunk * k
        so = m // block
        return so, (m - so * block) // chunk

    barrier = pltpu.get_barrier_semaphore()

    def tell(k, carry):
        t = lax.rem(me + k, n_red)
        pl.semaphore_signal(barrier, inc=1, device_id=((t // n_pan) * 2 + c, lax.rem(t, n_pan)),
                            device_id_type=MESH)
        return carry

    lax.fori_loop(1, n_red, tell, 0)
    pl.semaphore_signal(barrier, inc=1, device_id=core_peer, device_id_type=MESH)
    for k in range(n_row_chunks):
        so, po = row_owner(k)

        @pl.when(jnp.logical_or(so != s, po != p))
        def _():
            pl.semaphore_signal(barrier, inc=1, device_id=(so, po), device_id_type=MESH)

    positions = mics[...]
    part1 = positions.astype(jnp.bfloat16)
    rest = positions - part1.astype(jnp.float32)
    part2 = rest.astype(jnp.bfloat16)
    part3 = (rest - part2.astype(jnp.float32)).astype(jnp.bfloat16)
    n_mic = positions.shape[1]
    for b in range(n_split):
        listed = order[:, pl.ds(pl.multiple_of((2 * b + c) * block, LANES), block)]
        hot = (lax.broadcasted_iota(jnp.int32, (n_mic, block), 0) == listed)
        hot = jnp.where(hot, 1.0, 0.0).astype(jnp.bfloat16)
        chosen = sum(jnp.dot(q, hot, preferred_element_type=jnp.float32)
                     for q in (part1, part2, part3))
        for axis in range(3):
            scaled = chosen[axis:axis + 1] * (TURN if axis == 0 else TURN * BETA)
            for at in range(0, block, LANES):
                tile = jnp.broadcast_to(scaled[:, at:at + LANES], (LANES, LANES))
                micb[axis, pl.ds(b * block + at, LANES), :] = tile.T
    here = pl.ds(pl.multiple_of(y * half, LANES), half)
    for r, scale in enumerate((TURN, TURN * BETA, TURN * BETA, 1.0, 1.0 / BETA, 1.0 / BETA)):
        geo[r:r + 1, :] = geom[r:r + 1, here] * scale

    own_rows_sent = jnp.where(p_r == p, n_seg - 1, n_seg)
    if n_own < n_pan:
        own_rows_sent = jnp.where(owner, own_rows_sent, 0)
    pl.semaphore_wait(barrier, n_red + own_rows_sent)

    def seg_rows(index):
        return pl.ds(pl.multiple_of(index * segs_here, 16), segs_here)

    piece = half // pieces

    def y_copy(k, j):
        yy = lax.rem(y + k, n_split)
        start = pl.multiple_of(yy * half + j * piece, LANES)
        return pltpu.make_async_remote_copy(
            src_ref=src.at[:, :, :, pl.ds(start, piece)],
            dst_ref=src_buf.at[:, :, seg_rows(s), pl.ds(j * piece, piece)],
            send_sem=y_send.at[k - 1, j], recv_sem=y_recv.at[k - 1, j],
            device_id=(yy * 2 + c, p), device_id_type=MESH)

    def y_from(k):
        return lax.rem(y + n_split - k, n_split) * 2 + c

    def forward(k, j, cc):
        at = lax.rem(y + n_split - k, n_split) * 2 + cc
        ref = src_buf.at[:, :, seg_rows(at), pl.ds(j * piece, piece)]
        return pltpu.make_async_remote_copy(
            src_ref=ref, dst_ref=ref, send_sem=f_send.at[k - 1, j], recv_sem=f_recv.at[k - 1, j],
            device_id=core_peer, device_id_type=MESH)

    for j in range(pieces):
        for k in range(1, n_split):
            y_copy(k, j).start()
    core_copy = pltpu.make_async_remote_copy(
        src_ref=src.at[:, :, :, here], dst_ref=src_buf.at[:, :, seg_rows(s), :],
        send_sem=core_sems.at[0], recv_sem=core_sems.at[1],
        device_id=core_peer, device_id_type=MESH)
    core_copy.start()
    local_copy = pltpu.make_async_copy(
        src.at[:, :, :, here], src_buf.at[:, :, seg_rows(s), :], loc_sem.at[0])
    local_copy.start()

    mic_here = n_split * block
    body_rows = min(256, mic_here)
    parts = mic_here // body_rows

    def pairs(step, carry):
        lane = pl.multiple_of((step // parts) * LANES, LANES)
        base = lax.rem(step, parts) * body_rows
        panel = [jnp.broadcast_to(geo[r:r + 1, pl.ds(lane, LANES)], (SUB_ROWS, LANES))
                 for r in range(6)]
        for q in range(body_rows // SUB_ROWS):
            at = pl.ds(pl.multiple_of(base + q * SUB_ROWS, SUB_ROWS), SUB_ROWS)
            terms = pair_terms(micb[0, at, :], micb[1, at, :], micb[2, at, :], panel)
            for i in range(4):
                g_buf[i, at, pl.ds(lane, LANES)] = terms[i].astype(jnp.bfloat16)
        return carry

    steps = (piece // LANES) * parts
    for j in range(pieces):
        lax.fori_loop(j * steps, (j + 1) * steps, pairs, 0)
        for k in range(1, n_split):
            y_copy(k, j).wait_recv()
            forward(k, j, c).start()

    local_copy.wait()
    core_copy.wait()
    nt = (((1,), (1,)), ((), ()))
    for j in range(pieces):
        for k in range(1, n_split):
            y_copy(k, j).wait_send()
            forward(k, j, c).wait_send()
            forward(k, j, 1 - c).wait_recv()
        at = pl.ds(j * piece, piece)
        mono = jnp.concatenate([src_buf[0, 0, :, at], src_buf[1, 0, :, at]], axis=0)
        dipole = jnp.concatenate([src_buf[0, 1, :, at], src_buf[1, 1, :, at]], axis=0)
        for first, total in ((0, r1), (1, r2)):
            term = lax.dot_general(g_buf[first, :, at], mono, nt,
                                   preferred_element_type=jnp.float32)
            term += lax.dot_general(g_buf[first + 2, :, at], dipole, nt,
                                    preferred_element_type=jnp.float32)
            total[...] = term if j == 0 else total[...] + term

    n_all = n_seg * segs_here
    for b in range(n_split):
        band = pl.ds(b * block, block)
        spec[b, :, :n_all] = r1[band, :n_all] - r2[band, n_all:]
        spec[b, :, n_all:] = r1[band, n_all:] + r2[band, :n_all]

    def rs_copy(t):
        ty = t // n_pan
        tp = lax.rem(t, n_pan)
        return tp, pltpu.make_async_remote_copy(
            src_ref=spec.at[ty, pl.ds(pl.multiple_of(tp * chunk, 8), chunk)],
            dst_ref=rs_buf.at[me], send_sem=rs_send.at[t], recv_sem=rs_recv.at[me],
            device_id=(ty * 2 + c, tp), device_id_type=MESH)

    def each_rs(action):
        def go(k, carry):
            tp, copy = rs_copy(lax.rem(me + k, n_red))
            if n_own < n_pan:
                pl.when(tp < n_own)(lambda: action(copy))
            else:
                action(copy)
            return carry

        lax.fori_loop(1, n_red, go, 0)

    each_rs(lambda copy: copy.start())

    def own_slot(ref):
        return ref.at[pl.ds(pl.multiple_of(p * chunk, 8), chunk)]

    def col_copy(q):
        return pltpu.make_async_remote_copy(
            src_ref=own, dst_ref=own_slot(cols), send_sem=col_send.at[q], recv_sem=col_recv.at[p],
            device_id=(s, q), device_id_type=MESH)

    def row_copy(q):
        return pltpu.make_async_remote_copy(
            src_ref=own, dst_ref=rows.at[pl.ds(pl.multiple_of(row_slot * chunk, 8), chunk)],
            send_sem=row_send.at[q], recv_sem=row_recv.at[row_slot],
            device_id=(q, p_r), device_id_type=MESH)

    def each_col(action):
        def go(k, carry):
            action(lax.rem(p + k, n_pan))
            return carry

        lax.fori_loop(1, n_pan, go, 0)

    def each_row(action):
        for k in range(n_seg):
            q = lax.rem(s + k, n_seg)
            if k == 0:
                pl.when(p_r != p)(lambda: action(row_copy(q)))
            else:
                action(row_copy(q))

    def own_sum():
        rs_buf[me] = spec[y, pl.ds(pl.multiple_of(p * chunk, 8), chunk), :]

        def arrived(k, carry):
            t = lax.rem(me + k, n_red)
            pltpu.make_async_remote_copy(
                src_ref=rs_buf.at[t], dst_ref=rs_buf.at[t], send_sem=rs_send.at[t],
                recv_sem=rs_recv.at[t], device_id=core_peer, device_id_type=MESH).wait_recv()
            return carry

        lax.fori_loop(1, n_red, arrived, 0)
        own[...] = jnp.sum(rs_buf[...], axis=0)
        each_col(lambda q: col_copy(q).start())
        each_row(lambda copy: copy.start())
        cols[pl.ds(pl.multiple_of(p * chunk, 8), chunk), :] = own[...]

        @pl.when(p_r == p)
        def _():
            rows[pl.ds(pl.multiple_of(row_slot * chunk, 8), chunk), :] = own[...]

    def own_done():
        each_col(lambda q: col_copy(q).wait_send())
        each_row(lambda copy: copy.wait_send())

    if n_own < n_pan:
        pl.when(owner)(own_sum)
    else:
        own_sum()

    each_rs(lambda copy: copy.wait_send())

    def col_arrived(k, carry):
        q = lax.rem(p + k, n_pan)

        def wait():
            slot = cols.at[pl.ds(pl.multiple_of(q * chunk, 8), chunk)]
            pltpu.make_async_remote_copy(
                src_ref=slot, dst_ref=slot, send_sem=col_send.at[q], recv_sem=col_recv.at[q],
                device_id=core_peer, device_id_type=MESH).wait_recv()

        if n_own < n_pan:
            pl.when(q < n_own)(wait)
        else:
            wait()
        return carry

    lax.fori_loop(1, n_pan, col_arrived, 0)
    for k in range(n_row_chunks):
        so, po = row_owner(k)

        @pl.when(jnp.logical_or(so != s, po != p))
        def _():
            slot = rows.at[pl.ds(k * chunk, chunk)]
            pltpu.make_async_remote_copy(
                src_ref=slot, dst_ref=slot, send_sem=row_send.at[0], recv_sem=row_recv.at[k],
                device_id=core_peer, device_id_type=MESH).wait_recv()

    row_spec = rows[...]
    col_spec = cols[...]
    turned = jnp.concatenate([row_spec[:, n_all:], -row_spec[:, :n_all]], axis=1)
    highest = lax.Precision.HIGHEST
    out[0] = lax.dot_general(row_spec, col_spec, nt, precision=highest,
                             preferred_element_type=jnp.float32) * (1.0 / n_all)
    out[1] = lax.dot_general(turned, col_spec, nt, precision=highest,
                             preferred_element_type=jnp.float32) * (1.0 / n_all)
    if n_own < n_pan:
        pl.when(owner)(own_done)
    else:
        own_done()


def shards(sources, panel_geom, mic_pos, mic_order):
    n_seg = lax.axis_size("seg")
    n_pan = lax.axis_size("pan")
    segs_here = sources.shape[2]
    panels = sources.shape[3]
    n_mic = mic_pos.shape[1]
    n_split = n_seg // 2
    half = panels // n_split
    block = n_mic // n_seg
    chunk = max(8, block // n_pan)
    n_own = block // chunk
    rows_per = n_mic // n_pan
    n_red = n_split * n_pan
    width = 2 * n_seg * segs_here
    pieces = 4
    cfg = (n_seg, n_pan, segs_here, half, block, chunk, n_own, rows_per, pieces)
    f32, bf16 = jnp.float32, jnp.bfloat16
    dma = pltpu.SemaphoreType.DMA
    vmem = pl.BlockSpec(memory_space=pltpu.VMEM)
    mic_here = n_split * block
    return pl.pallas_call(
        functools.partial(kernel, cfg),
        out_shape=jax.ShapeDtypeStruct((2, rows_per, block), f32),
        in_specs=[pl.BlockSpec(memory_space=pl.ANY), vmem, vmem, vmem],
        out_specs=vmem,
        scratch_shapes=[
            pltpu.VMEM((2, 2, n_seg * segs_here, half), bf16),
            pltpu.VMEM((8, half), f32),
            pltpu.VMEM((3, mic_here, LANES), f32),
            pltpu.VMEM((4, mic_here, half), bf16),
            pltpu.VMEM((mic_here, width), f32),
            pltpu.VMEM((mic_here, width), f32),
            pltpu.VMEM((n_split, block, width), f32),
            pltpu.VMEM((n_red, chunk, width), f32),
            pltpu.VMEM((chunk, width), f32),
            pltpu.VMEM((block, width), f32),
            pltpu.VMEM((rows_per, width), f32),
            dma((1,)), dma((2,)),
            dma((n_split - 1, pieces)), dma((n_split - 1, pieces)),
            dma((n_split - 1, pieces)), dma((n_split - 1, pieces)),
            dma((n_red,)), dma((n_red,)),
            dma((n_pan,)), dma((n_pan,)),
            dma((n_seg,)), dma((rows_per // chunk,)),
        ],
        compiler_params=pltpu.CompilerParams(
            collective_id=0, has_side_effects=True, vmem_limit_bytes=48 * 2**20),
        cost_estimate=pl.CostEstimate(
            flops=2 * 4 * mic_here * half * width, bytes_accessed=2**21,
            transcendentals=mic_here * half),
    )(sources, panel_geom, mic_pos, mic_order.reshape(1, n_mic))


def solution(mesh):
    placed = (P(None, None, "seg", "pan"), P(None, "pan"), P(), P())
    return jax.shard_map(
        shards, mesh=mesh, in_specs=placed, out_specs=P(None, "pan", "seg"), check_vma=False
    )
```

time: 396 us -> 46.6 us (0.12)
  other arithmetic: 201 us -> 0 us
  waiting for transfers between devices: 96.9 us -> 0 us
  matrix products: 45.4 us -> 0 us
  Pallas kernels: 0 us -> 42 us
  local copies, waits for them, and re-layouts: 35.9 us -> 4.28 us
  between operations: 13.5 us -> 0.01 us
    another operation x17 -> x0, other arithmetic: 198 us -> none
    psum x1 -> x0, waiting for transfers between devices: 72.5 us -> none  [summed_spectra(): return lax.psum(local_terms, 'pan')]
    dot_general x20 -> x0, matrix products: 45.4 us -> none  [the longest x16 41.1 us: step(): jnp.dot(kernel_block(mics, geometry), weights, preferred_element_type=jnp...]
    pallas_call x0 -> x1, Pallas kernels: none -> 42 us  [shards(): pl.pallas_call(functools.partial(kernel, cfg), out_shape=jax.ShapeDtypeSt...]
    reduce_scatter x1 -> x0, waiting for transfers between devices: 24.3 us -> none  [shards(): lax.psum_scatter(partial_csm, 'seg', scatter_dimension=2, tiled=True)]
    slice x32 -> x0, local copies, waits for them, and re-layouts: 15.7 us -> none  [kernel_block(): dx = mics[0][:, None] - geometry[0][None, :]]
    transpose x16 -> x0, local copies, waits for them, and re-layouts: 13.5 us -> none  [block_weights(): swapped = jnp.transpose(piece, (0, 1, 3, 2))]
  transfers between devices with their start and end apart: 2 -> 0, of which waited for: 2 -> 0; matrix products, arithmetic and copies ran while one was open for 0% -> 0% of each run, Pallas kernels for 0% -> 0%
where the time goes in v1:
time: 46.6 us; the launch traced here: 46.3 us
  Pallas kernels  42 us (90%)
  local copies, waits for them, and re-layouts  4.28 us (9%)
    pallas_call x1, Pallas kernels, shards(): pl.pallas_call(functools.partial(kernel, cfg), out_shape=jax.ShapeDtypeSt...  42 us
    unnamed x9, local copies, waits for them, and re-layouts  4.28 us

profile of v1, /device:TPU:0, one launch (start us, length us, event | category | flops | bytes accessed | tf_op | source)
XLA Modules:
  0.0 46.3 jit_solution(14817511241254169072)
XLA Ops:
  0.0 0.0 copy-start
  0.0 1.2 %copy-done = bf16[2,2,16,8192]{3,2,1,0:T(8,128)(2,1)S(1)} copy-done((bf16[2,2,16,8192]{3,2,1,0:T(8,128)(2,1)S(1)}, bf16[2,2,16,8192]{3,2,1,0:T(8,128)(2,1)}, u32[]{:S(2)}) %copy-start) | copy-done | bytes 1048600
  1.2 0.0 copy-start.1
  1.2 0.9 %copy-done.1 = f32[6,8192]{1,0:T(8,128)S(1)} copy-done((f32[6,8192]{1,0:T(8,128)S(1)}, f32[6,8192]{1,0:T(8,128)}, u32[]{:S(2)}) %copy-start.1) | copy-done | bytes 196632
  2.2 0.0 copy-start.2
  2.2 0.7 %copy-done.2 = f32[3,1024]{1,0:T(4,128)S(1)} copy-done((f32[3,1024]{1,0:T(4,128)S(1)}, f32[3,1024]{1,0:T(4,128)}, u32[]{:S(2)}) %copy-start.2) | copy-done | bytes 12312
  2.9 0.0 copy-start.3
  2.9 0.7 %copy-done.3 = s32[1024]{0:T(1024)S(1)} copy-done((s32[1024]{0:T(1024)S(1)}, s32[1024]{0:T(1024)}, u32[]{:S(2)}) %copy-start.3) | copy-done | bytes 4120
  3.6 42.0 %shard_map.46 = f32[2,128,256]{2,1,0:T(8,128)S(1)} custom-call(bf16[2,2,16,8192]{3,2,1,0:T(8,128)(2,1)S(1)} %copy-done, f32[6,8192]{1,0:T(8,128)S(1)} %copy-done.1, f32[3,1024]{1,0:T(4,128)S(1)} %copy-done.2, s32[1,1024]{1,0:T(1,128)S(1)} %bitcast.1), custom_call_target="tpu_custom_call" | custom-call | flops 2147483648 | bytes 2097152 | tf_op jit(solution)/shard_map/pallas_call | solution.py:361
  45.6 0.7 %copy.6 = f32[2,128,256]{2,1,0:T(8,128)} copy(f32[2,128,256]{2,1,0:T(8,128)S(1)} %shard_map.46) | data formatting | bytes 524288
Async XLA Ops:
  0.0 1.2 %copy-start = (bf16[2,2,16,8192]{3,2,1,0:T(8,128)(2,1)S(1)}, bf16[2,2,16,8192]{3,2,1,0:T(8,128)(2,1)}, u32[]{:S(2)}) copy-start(bf16[2,2,16,8192]{3,2,1,0:T(8,128)(2,1)} %src.1) | copy-start | bytes 3145732
  1.2 0.9 %copy-start.1 = (f32[6,8192]{1,0:T(8,128)S(1)}, f32[6,8192]{1,0:T(8,128)}, u32[]{:S(2)}) copy-start(f32[6,8192]{1,0:T(8,128)} %geom.1) | copy-start | bytes 589828
  2.2 0.7 %copy-start.2 = (f32[3,1024]{1,0:T(4,128)S(1)}, f32[3,1024]{1,0:T(4,128)}, u32[]{:S(2)}) copy-start(f32[3,1024]{1,0:T(4,128)} %mics.1) | copy-start | bytes 36868
  2.9 0.7 %copy-start.3 = (s32[1024]{0:T(1024)S(1)}, s32[1024]{0:T(1024)}, u32[]{:S(2)}) copy-start(s32[1024]{0:T(1024)} %param.7) | copy-start | bytes 12292

commit v2 on v1

--- a/solution.py
+++ b/solution.py
@@ -16,6 +16,7 @@
 MESH = pl.DeviceIdType.MESH
 LANES = 128
 SUB_ROWS = 32
+LAG = 3
 TURN = wave_number / (beta_sq * 2.0 * math.pi)
 BETA = math.sqrt(beta_sq)
 
@@ -33,7 +34,7 @@
 
 
 ROOT2 = math.sqrt(2.0)
-SIN_COEF = fit(lambda x: ROOT2 * np.sin(math.pi * x), 4, 0.5, True)
+SIN_COEF = fit(lambda x: -ROOT2 * np.sin(math.pi * x), 3, 0.5, True)
 COS_COEF = fit(lambda x: ROOT2 * np.cos(math.pi * x), 4, 0.5, False)
 
 
@@ -60,16 +61,16 @@
     c = horner(COS_COEF, u)
     amplitude = inv * (TURN / (4.0 * math.pi))
     green_re = amplitude * (1.0 - s * s)
-    green_im_neg = amplitude * (s * c)
+    green_im = amplitude * (s * c)
     normal_part = (dx * n0 + (dy * n1 + dz * n2)) * inv
     near = inv * (TURN / wave_number)
-    dip_re = normal_part * (near * green_re + green_im_neg)
-    dip_im = normal_part * (green_re - near * green_im_neg)
-    return green_re, -green_im_neg, dip_re, dip_im
-
-
-def kernel(cfg, src, geom, mics, order, out, src_buf, geo, micb, g_buf, r1, r2, spec,
-           rs_buf, own, cols, rows, loc_sem, core_sems, y_send, y_recv, f_send, f_recv,
+    dip_re = normal_part * (near * green_re - green_im)
+    dip_im = normal_part * (near * green_im + green_re)
+    return green_re, green_im, dip_re, dip_im
+
+
+def kernel(cfg, src, geom_hbm, mics_hbm, order_hbm, out, src_buf, geom, mics, order, geo, micb,
+           g_even, g_odd, r1, r2, spec, rs_buf, own, cols, rows, loc_sem, core_sems, y_send, y_recv, f_send, f_recv,
            rs_send, rs_recv, col_send, col_recv, row_send, row_recv):
     n_seg, n_pan, segs_here, half, block, chunk, n_own, rows_per, pieces = cfg
     n_split = n_seg // 2
@@ -107,6 +108,17 @@
         @pl.when(jnp.logical_or(so != s, po != p))
         def _():
             pl.semaphore_signal(barrier, inc=1, device_id=(so, po), device_id_type=MESH)
+
+    here = pl.ds(pl.multiple_of(y * half, LANES), half)
+    fetches = [
+        pltpu.make_async_copy(order_hbm, order, loc_sem.at[1]),
+        pltpu.make_async_copy(mics_hbm, mics, loc_sem.at[2]),
+        pltpu.make_async_copy(geom_hbm.at[:, here], geom, loc_sem.at[3]),
+    ]
+    for fetch in fetches:
+        fetch.start()
+    for fetch in fetches:
+        fetch.wait()
 
     positions = mics[...]
     part1 = positions.astype(jnp.bfloat16)
@@ -125,9 +137,10 @@
             for at in range(0, block, LANES):
                 tile = jnp.broadcast_to(scaled[:, at:at + LANES], (LANES, LANES))
                 micb[axis, pl.ds(b * block + at, LANES), :] = tile.T
-    here = pl.ds(pl.multiple_of(y * half, LANES), half)
+    r1[...] = jnp.zeros_like(r1)
+    r2[...] = jnp.zeros_like(r2)
     for r, scale in enumerate((TURN, TURN * BETA, TURN * BETA, 1.0, 1.0 / BETA, 1.0 / BETA)):
-        geo[r:r + 1, :] = geom[r:r + 1, here] * scale
+        geo[r:r + 1, :] = geom[r:r + 1, :] * scale
 
     own_rows_sent = jnp.where(p_r == p, n_seg - 1, n_seg)
     if n_own < n_pan:
@@ -144,7 +157,7 @@
         start = pl.multiple_of(yy * half + j * piece, LANES)
         return pltpu.make_async_remote_copy(
             src_ref=src.at[:, :, :, pl.ds(start, piece)],
-            dst_ref=src_buf.at[:, :, seg_rows(s), pl.ds(j * piece, piece)],
+            dst_ref=src_buf.at[:, :, seg_rows(s), pl.ds(pl.multiple_of(j * piece, LANES), piece)],
             send_sem=y_send.at[k - 1, j], recv_sem=y_recv.at[k - 1, j],
             device_id=(yy * 2 + c, p), device_id_type=MESH)
 
@@ -153,14 +166,17 @@
 
     def forward(k, j, cc):
         at = lax.rem(y + n_split - k, n_split) * 2 + cc
-        ref = src_buf.at[:, :, seg_rows(at), pl.ds(j * piece, piece)]
+        ref = src_buf.at[:, :, seg_rows(at), pl.ds(pl.multiple_of(j * piece, LANES), piece)]
         return pltpu.make_async_remote_copy(
             src_ref=ref, dst_ref=ref, send_sem=f_send.at[k - 1, j], recv_sem=f_recv.at[k - 1, j],
             device_id=core_peer, device_id_type=MESH)
 
-    for j in range(pieces):
+    def start_y(j, carry):
         for k in range(1, n_split):
             y_copy(k, j).start()
+        return carry
+
+    lax.fori_loop(0, pieces, start_y, 0)
     core_copy = pltpu.make_async_remote_copy(
         src_ref=src.at[:, :, :, here], dst_ref=src_buf.at[:, :, seg_rows(s), :],
         send_sem=core_sems.at[0], recv_sem=core_sems.at[1],
@@ -172,44 +188,84 @@
 
     mic_here = n_split * block
     body_rows = min(256, mic_here)
-    parts = mic_here // body_rows
-
-    def pairs(step, carry):
-        lane = pl.multiple_of((step // parts) * LANES, LANES)
-        base = lax.rem(step, parts) * body_rows
-        panel = [jnp.broadcast_to(geo[r:r + 1, pl.ds(lane, LANES)], (SUB_ROWS, LANES))
-                 for r in range(6)]
-        for q in range(body_rows // SUB_ROWS):
-            at = pl.ds(pl.multiple_of(base + q * SUB_ROWS, SUB_ROWS), SUB_ROWS)
-            terms = pair_terms(micb[0, at, :], micb[1, at, :], micb[2, at, :], panel)
-            for i in range(4):
-                g_buf[i, at, pl.ds(lane, LANES)] = terms[i].astype(jnp.bfloat16)
-        return carry
-
-    steps = (piece // LANES) * parts
-    for j in range(pieces):
-        lax.fori_loop(j * steps, (j + 1) * steps, pairs, 0)
+    nt = (((1,), (1,)), ((), ()))
+
+    def slot_lanes(j):
+        return (j // 2) * piece
+
+    def products(j, g_ref, band):
+        at = pl.ds(pl.multiple_of(j * piece, LANES), piece)
+        slot = pl.ds(pl.multiple_of(slot_lanes(j), LANES), piece)
+        mono = jnp.concatenate([src_buf[0, 0, :, at], src_buf[1, 0, :, at]], axis=0)
+        dipole = jnp.concatenate([src_buf[0, 1, :, at], src_buf[1, 1, :, at]], axis=0)
+        for first, total in ((0, r1), (1, r2)):
+            term = lax.dot_general(g_ref[first, band, slot], mono, nt,
+                                   preferred_element_type=jnp.float32)
+            term += lax.dot_general(g_ref[first + 2, band, slot], dipole, nt,
+                                    preferred_element_type=jnp.float32)
+            total[band, :] += term
+
+    def pairs(j, g_ref, base):
+        for lane in range(0, piece, LANES):
+            read = pl.ds(pl.multiple_of(j * piece + lane, LANES), LANES)
+            write = pl.ds(pl.multiple_of(slot_lanes(j) + lane, LANES), LANES)
+            panel = [jnp.broadcast_to(geo[r:r + 1, read], (SUB_ROWS, LANES)) for r in range(6)]
+            for q in range(body_rows // SUB_ROWS):
+                at = pl.ds(pl.multiple_of(base + q * SUB_ROWS, SUB_ROWS), SUB_ROWS)
+                terms = pair_terms(micb[0, at, :], micb[1, at, :], micb[2, at, :], panel)
+                for i in range(4):
+                    g_ref[i, at, write] = terms[i].astype(jnp.bfloat16)
+
+    g_refs = (g_even, g_odd)
+
+    def unit(j, parity, with_pairs, with_products):
+        if with_products:
+            for k in range(1, n_split):
+                forward(k, j - LAG, 1 - c).wait_recv()
+
+        def band_step(h, carry):
+            base = pl.multiple_of(h * body_rows, body_rows)
+            if with_products:
+                products(j - LAG, g_refs[1 - parity], pl.ds(base, body_rows))
+            if with_pairs:
+                pairs(j, g_refs[parity], base)
+            return carry
+
+        lax.fori_loop(0, mic_here // body_rows, band_step, 0)
+
+    def pass_on(j):
         for k in range(1, n_split):
             y_copy(k, j).wait_recv()
             forward(k, j, c).start()
 
+    for j in range(LAG):
+        unit(j, j % 2, True, False)
+        if j > 0:
+            pass_on(j - 1)
     local_copy.wait()
     core_copy.wait()
-    nt = (((1,), (1,)), ((), ()))
-    for j in range(pieces):
+
+    def two_units(i, carry):
+        for extra in range(2):
+            j = LAG + 2 * i + extra
+            unit(j, (LAG + extra) % 2, True, True)
+            pass_on(j - 1)
+        return carry
+
+    lax.fori_loop(0, (pieces - LAG - 1) // 2, two_units, 0)
+    unit(pieces - 1, (pieces - 1) % 2, True, True)
+    pass_on(pieces - 2)
+    pass_on(pieces - 1)
+    for j in range(pieces, pieces + LAG):
+        unit(j, j % 2, False, True)
+
+    def sent(j, carry):
         for k in range(1, n_split):
             y_copy(k, j).wait_send()
             forward(k, j, c).wait_send()
-            forward(k, j, 1 - c).wait_recv()
-        at = pl.ds(j * piece, piece)
-        mono = jnp.concatenate([src_buf[0, 0, :, at], src_buf[1, 0, :, at]], axis=0)
-        dipole = jnp.concatenate([src_buf[0, 1, :, at], src_buf[1, 1, :, at]], axis=0)
-        for first, total in ((0, r1), (1, r2)):
-            term = lax.dot_general(g_buf[first, :, at], mono, nt,
-                                   preferred_element_type=jnp.float32)
-            term += lax.dot_general(g_buf[first + 2, :, at], dipole, nt,
-                                    preferred_element_type=jnp.float32)
-            total[...] = term if j == 0 else total[...] + term
+        return carry
+
+    lax.fori_loop(0, pieces, sent, 0)
 
     n_all = n_seg * segs_here
     for b in range(n_split):
@@ -352,7 +408,7 @@
     rows_per = n_mic // n_pan
     n_red = n_split * n_pan
     width = 2 * n_seg * segs_here
-    pieces = 4
+    pieces = half // 256
     cfg = (n_seg, n_pan, segs_here, half, block, chunk, n_own, rows_per, pieces)
     f32, bf16 = jnp.float32, jnp.bfloat16
     dma = pltpu.SemaphoreType.DMA
@@ -361,13 +417,17 @@
     return pl.pallas_call(
         functools.partial(kernel, cfg),
         out_shape=jax.ShapeDtypeStruct((2, rows_per, block), f32),
-        in_specs=[pl.BlockSpec(memory_space=pl.ANY), vmem, vmem, vmem],
+        in_specs=[pl.BlockSpec(memory_space=pltpu.HBM)] * 4,
         out_specs=vmem,
         scratch_shapes=[
             pltpu.VMEM((2, 2, n_seg * segs_here, half), bf16),
+            pltpu.VMEM((6, half), f32),
+            pltpu.VMEM((3, n_mic), f32),
+            pltpu.VMEM((1, n_mic), jnp.int32),
             pltpu.VMEM((8, half), f32),
             pltpu.VMEM((3, mic_here, LANES), f32),
-            pltpu.VMEM((4, mic_here, half), bf16),
+            pltpu.VMEM((4, mic_here, half // 2), bf16),
+            pltpu.VMEM((4, mic_here, half // 2), bf16),
             pltpu.VMEM((mic_here, width), f32),
             pltpu.VMEM((mic_here, width), f32),
             pltpu.VMEM((n_split, block, width), f32),
@@ -375,7 +435,7 @@
             pltpu.VMEM((chunk, width), f32),
             pltpu.VMEM((block, width), f32),
             pltpu.VMEM((rows_per, width), f32),
-            dma((1,)), dma((2,)),
+            dma((4,)), dma((2,)),
             dma((n_split - 1, pieces)), dma((n_split - 1, pieces)),
             dma((n_split - 1, pieces)), dma((n_split - 1, pieces)),
             dma((n_red,)), dma((n_red,)),

time: 46.6 us -> 54.7 us (1.17)
  Pallas kernels: 42 us -> 49.8 us
    pallas_call x1, Pallas kernels: 42 us -> 49.8 us  [shards(): pl.pallas_call(functools.partial(kernel, cfg), out_shape=jax.ShapeDtypeSt...]
where the time goes in v2:
time: 54.7 us; the launch traced here: 54.1 us
  Pallas kernels  49.8 us (91%)
  local copies, waits for them, and re-layouts  4.28 us (8%)
    pallas_call x1, Pallas kernels, shards(): pl.pallas_call(functools.partial(kernel, cfg), out_shape=jax.ShapeDtypeSt...  49.8 us
    unnamed x9, local copies, waits for them, and re-layouts  4.28 us

profile of v2, /device:TPU:0, one launch (start us, length us, event | category | flops | bytes accessed | tf_op | source)
XLA Modules:
  0.0 54.1 jit_solution(5178755162435334453)
XLA Ops:
  0.0 0.0 copy-start
  0.0 1.2 %copy-done = bf16[2,2,16,8192]{3,2,1,0:T(8,128)(2,1)S(1)} copy-done((bf16[2,2,16,8192]{3,2,1,0:T(8,128)(2,1)S(1)}, bf16[2,2,16,8192]{3,2,1,0:T(8,128)(2,1)}, u32[]{:S(2)}) %copy-start) | copy-done | bytes 1048600
  1.2 0.0 copy-start.1
  1.2 0.9 %copy-done.1 = f32[6,8192]{1,0:T(8,128)S(1)} copy-done((f32[6,8192]{1,0:T(8,128)S(1)}, f32[6,8192]{1,0:T(8,128)}, u32[]{:S(2)}) %copy-start.1) | copy-done | bytes 196632
  2.2 0.0 copy-start.2
  2.2 0.7 %copy-done.2 = f32[3,1024]{1,0:T(4,128)S(1)} copy-done((f32[3,1024]{1,0:T(4,128)S(1)}, f32[3,1024]{1,0:T(4,128)}, u32[]{:S(2)}) %copy-start.2) | copy-done | bytes 12312
  2.9 0.0 copy-start.3
  2.9 0.7 %copy-done.3 = s32[1024]{0:T(1024)S(1)} copy-done((s32[1024]{0:T(1024)S(1)}, s32[1024]{0:T(1024)}, u32[]{:S(2)}) %copy-start.3) | copy-done | bytes 4120
  3.6 49.8 %shard_map.46 = f32[2,128,256]{2,1,0:T(8,128)S(1)} custom-call(bf16[2,2,16,8192]{3,2,1,0:T(8,128)(2,1)S(1)} %copy-done, f32[6,8192]{1,0:T(8,128)S(1)} %copy-done.1, f32[3,1024]{1,0:T(4,128)S(1)} %copy-done.2, s32[1,1024]{1,0:T(1,128)S(1)} %bitcast.1), custom_call_target="tpu_custom_call" | custom-call | flops 2147483648 | bytes 2097152 | tf_op jit(solution)/shard_map/pallas_call | solution.py:417
  53.4 0.7 %copy.6 = f32[2,128,256]{2,1,0:T(8,128)} copy(f32[2,128,256]{2,1,0:T(8,128)S(1)} %shard_map.46) | data formatting | bytes 524288
Async XLA Ops:
  0.0 1.2 %copy-start = (bf16[2,2,16,8192]{3,2,1,0:T(8,128)(2,1)S(1)}, bf16[2,2,16,8192]{3,2,1,0:T(8,128)(2,1)}, u32[]{:S(2)}) copy-start(bf16[2,2,16,8192]{3,2,1,0:T(8,128)(2,1)} %src.1) | copy-start | bytes 3145732
  1.2 0.9 %copy-start.1 = (f32[6,8192]{1,0:T(8,128)S(1)}, f32[6,8192]{1,0:T(8,128)}, u32[]{:S(2)}) copy-start(f32[6,8192]{1,0:T(8,128)} %geom_hbm.1) | copy-start | bytes 589828
  2.2 0.7 %copy-start.2 = (f32[3,1024]{1,0:T(4,128)S(1)}, f32[3,1024]{1,0:T(4,128)}, u32[]{:S(2)}) copy-start(f32[3,1024]{1,0:T(4,128)} %mics_hbm.1) | copy-start | bytes 36868
  2.9 0.7 %copy-start.3 = (s32[1024]{0:T(1024)S(1)}, s32[1024]{0:T(1024)}, u32[]{:S(2)}) copy-start(s32[1024]{0:T(1024)} %param.7) | copy-start | bytes 12292

commit v3 on v1

--- a/solution.py
+++ b/solution.py
@@ -33,7 +33,7 @@
 
 
 ROOT2 = math.sqrt(2.0)
-SIN_COEF = fit(lambda x: ROOT2 * np.sin(math.pi * x), 4, 0.5, True)
+SIN_COEF = fit(lambda x: -ROOT2 * np.sin(math.pi * x), 3, 0.5, True)
 COS_COEF = fit(lambda x: ROOT2 * np.cos(math.pi * x), 4, 0.5, False)
 
 
@@ -60,16 +60,16 @@
     c = horner(COS_COEF, u)
     amplitude = inv * (TURN / (4.0 * math.pi))
     green_re = amplitude * (1.0 - s * s)
-    green_im_neg = amplitude * (s * c)
+    green_im = amplitude * (s * c)
     normal_part = (dx * n0 + (dy * n1 + dz * n2)) * inv
     near = inv * (TURN / wave_number)
-    dip_re = normal_part * (near * green_re + green_im_neg)
-    dip_im = normal_part * (green_re - near * green_im_neg)
-    return green_re, -green_im_neg, dip_re, dip_im
-
-
-def kernel(cfg, src, geom, mics, order, out, src_buf, geo, micb, g_buf, r1, r2, spec,
-           rs_buf, own, cols, rows, loc_sem, core_sems, y_send, y_recv, f_send, f_recv,
+    dip_re = normal_part * (near * green_re - green_im)
+    dip_im = normal_part * (near * green_im + green_re)
+    return green_re, green_im, dip_re, dip_im
+
+
+def kernel(cfg, src, geom_hbm, mics_hbm, order_hbm, out, src_buf, geom, mics, order, geo, micb,
+           g_buf, r1, r2, spec, rs_buf, own, cols, rows, loc_sem, core_sems, y_send, y_recv, f_send, f_recv,
            rs_send, rs_recv, col_send, col_recv, row_send, row_recv):
     n_seg, n_pan, segs_here, half, block, chunk, n_own, rows_per, pieces = cfg
     n_split = n_seg // 2
@@ -107,6 +107,17 @@
         @pl.when(jnp.logical_or(so != s, po != p))
         def _():
             pl.semaphore_signal(barrier, inc=1, device_id=(so, po), device_id_type=MESH)
+
+    here = pl.ds(pl.multiple_of(y * half, LANES), half)
+    fetches = [
+        pltpu.make_async_copy(order_hbm, order, loc_sem.at[1]),
+        pltpu.make_async_copy(mics_hbm, mics, loc_sem.at[2]),
+        pltpu.make_async_copy(geom_hbm.at[:, here], geom, loc_sem.at[3]),
+    ]
+    for fetch in fetches:
+        fetch.start()
+    for fetch in fetches:
+        fetch.wait()
 
     positions = mics[...]
     part1 = positions.astype(jnp.bfloat16)
@@ -125,9 +136,8 @@
             for at in range(0, block, LANES):
                 tile = jnp.broadcast_to(scaled[:, at:at + LANES], (LANES, LANES))
                 micb[axis, pl.ds(b * block + at, LANES), :] = tile.T
-    here = pl.ds(pl.multiple_of(y * half, LANES), half)
     for r, scale in enumerate((TURN, TURN * BETA, TURN * BETA, 1.0, 1.0 / BETA, 1.0 / BETA)):
-        geo[r:r + 1, :] = geom[r:r + 1, here] * scale
+        geo[r:r + 1, :] = geom[r:r + 1, :] * scale
 
     own_rows_sent = jnp.where(p_r == p, n_seg - 1, n_seg)
     if n_own < n_pan:
@@ -144,7 +154,7 @@
         start = pl.multiple_of(yy * half + j * piece, LANES)
         return pltpu.make_async_remote_copy(
             src_ref=src.at[:, :, :, pl.ds(start, piece)],
-            dst_ref=src_buf.at[:, :, seg_rows(s), pl.ds(j * piece, piece)],
+            dst_ref=src_buf.at[:, :, seg_rows(s), pl.ds(pl.multiple_of(j * piece, LANES), piece)],
             send_sem=y_send.at[k - 1, j], recv_sem=y_recv.at[k - 1, j],
             device_id=(yy * 2 + c, p), device_id_type=MESH)
 
@@ -153,14 +163,17 @@
 
     def forward(k, j, cc):
         at = lax.rem(y + n_split - k, n_split) * 2 + cc
-        ref = src_buf.at[:, :, seg_rows(at), pl.ds(j * piece, piece)]
+        ref = src_buf.at[:, :, seg_rows(at), pl.ds(pl.multiple_of(j * piece, LANES), piece)]
         return pltpu.make_async_remote_copy(
             src_ref=ref, dst_ref=ref, send_sem=f_send.at[k - 1, j], recv_sem=f_recv.at[k - 1, j],
             device_id=core_peer, device_id_type=MESH)
 
-    for j in range(pieces):
+    def start_y(j, carry):
         for k in range(1, n_split):
             y_copy(k, j).start()
+        return carry
+
+    lax.fori_loop(0, pieces, start_y, 0)
     core_copy = pltpu.make_async_remote_copy(
         src_ref=src.at[:, :, :, here], dst_ref=src_buf.at[:, :, seg_rows(s), :],
         send_sem=core_sems.at[0], recv_sem=core_sems.at[1],
@@ -172,6 +185,8 @@
 
     mic_here = n_split * block
     body_rows = min(256, mic_here)
+    nt = (((1,), (1,)), ((), ()))
+
     parts = mic_here // body_rows
 
     def pairs(step, carry):
@@ -195,7 +210,6 @@
 
     local_copy.wait()
     core_copy.wait()
-    nt = (((1,), (1,)), ((), ()))
     for j in range(pieces):
         for k in range(1, n_split):
             y_copy(k, j).wait_send()
@@ -361,10 +375,13 @@
     return pl.pallas_call(
         functools.partial(kernel, cfg),
         out_shape=jax.ShapeDtypeStruct((2, rows_per, block), f32),
-        in_specs=[pl.BlockSpec(memory_space=pl.ANY), vmem, vmem, vmem],
+        in_specs=[pl.BlockSpec(memory_space=pltpu.HBM)] * 4,
         out_specs=vmem,
         scratch_shapes=[
             pltpu.VMEM((2, 2, n_seg * segs_here, half), bf16),
+            pltpu.VMEM((6, half), f32),
+            pltpu.VMEM((3, n_mic), f32),
+            pltpu.VMEM((1, n_mic), jnp.int32),
             pltpu.VMEM((8, half), f32),
             pltpu.VMEM((3, mic_here, LANES), f32),
             pltpu.VMEM((4, mic_here, half), bf16),
@@ -375,7 +392,7 @@
             pltpu.VMEM((chunk, width), f32),
             pltpu.VMEM((block, width), f32),
             pltpu.VMEM((rows_per, width), f32),
-            dma((1,)), dma((2,)),
+            dma((4,)), dma((2,)),
             dma((n_split - 1, pieces)), dma((n_split - 1, pieces)),
             dma((n_split - 1, pieces)), dma((n_split - 1, pieces)),
             dma((n_red,)), dma((n_red,)),

time: 46.6 us -> 46.1 us (0.989)
  no operation moved by 1% of the time
where the time goes in v3:
time: 46.1 us; the launch traced here: 45.9 us
  Pallas kernels  41.6 us (90%)
  local copies, waits for them, and re-layouts  4.28 us (9%)
    pallas_call x1, Pallas kernels, shards(): pl.pallas_call(functools.partial(kernel, cfg), out_shape=jax.ShapeDtypeSt...  41.6 us
    unnamed x9, local copies, waits for them, and re-layouts  4.28 us

profile of v3, /device:TPU:0, one launch (start us, length us, event | category | flops | bytes accessed | tf_op | source)
XLA Modules:
  0.0 45.9 jit_solution(5570802277098805284)
XLA Ops:
  0.0 0.0 copy-start
  0.0 1.2 %copy-done = bf16[2,2,16,8192]{3,2,1,0:T(8,128)(2,1)S(1)} copy-done((bf16[2,2,16,8192]{3,2,1,0:T(8,128)(2,1)S(1)}, bf16[2,2,16,8192]{3,2,1,0:T(8,128)(2,1)}, u32[]{:S(2)}) %copy-start) | copy-done | bytes 1048600
  1.2 0.0 copy-start.1
  1.2 0.9 %copy-done.1 = f32[6,8192]{1,0:T(8,128)S(1)} copy-done((f32[6,8192]{1,0:T(8,128)S(1)}, f32[6,8192]{1,0:T(8,128)}, u32[]{:S(2)}) %copy-start.1) | copy-done | bytes 196632
  2.2 0.0 copy-start.2
  2.2 0.7 %copy-done.2 = f32[3,1024]{1,0:T(4,128)S(1)} copy-done((f32[3,1024]{1,0:T(4,128)S(1)}, f32[3,1024]{1,0:T(4,128)}, u32[]{:S(2)}) %copy-start.2) | copy-done | bytes 12312
  2.9 0.0 copy-start.3
  2.9 0.7 %copy-done.3 = s32[1024]{0:T(1024)S(1)} copy-done((s32[1024]{0:T(1024)S(1)}, s32[1024]{0:T(1024)}, u32[]{:S(2)}) %copy-start.3) | copy-done | bytes 4120
  3.6 41.6 %shard_map.46 = f32[2,128,256]{2,1,0:T(8,128)S(1)} custom-call(bf16[2,2,16,8192]{3,2,1,0:T(8,128)(2,1)S(1)} %copy-done, f32[6,8192]{1,0:T(8,128)S(1)} %copy-done.1, f32[3,1024]{1,0:T(4,128)S(1)} %copy-done.2, s32[1,1024]{1,0:T(1,128)S(1)} %bitcast.1), custom_call_target="tpu_custom_call" | custom-call | flops 2147483648 | bytes 2097152 | tf_op jit(solution)/shard_map/pallas_call | solution.py:375
  45.2 0.7 %copy.6 = f32[2,128,256]{2,1,0:T(8,128)} copy(f32[2,128,256]{2,1,0:T(8,128)S(1)} %shard_map.46) | data formatting | bytes 524288
Async XLA Ops:
  0.0 1.2 %copy-start = (bf16[2,2,16,8192]{3,2,1,0:T(8,128)(2,1)S(1)}, bf16[2,2,16,8192]{3,2,1,0:T(8,128)(2,1)}, u32[]{:S(2)}) copy-start(bf16[2,2,16,8192]{3,2,1,0:T(8,128)(2,1)} %src.1) | copy-start | bytes 3145732
  1.2 0.9 %copy-start.1 = (f32[6,8192]{1,0:T(8,128)S(1)}, f32[6,8192]{1,0:T(8,128)}, u32[]{:S(2)}) copy-start(f32[6,8192]{1,0:T(8,128)} %geom_hbm.1) | copy-start | bytes 589828
  2.2 0.7 %copy-start.2 = (f32[3,1024]{1,0:T(4,128)S(1)}, f32[3,1024]{1,0:T(4,128)}, u32[]{:S(2)}) copy-start(f32[3,1024]{1,0:T(4,128)} %mics_hbm.1) | copy-start | bytes 36868
  2.9 0.7 %copy-start.3 = (s32[1024]{0:T(1024)S(1)}, s32[1024]{0:T(1024)}, u32[]{:S(2)}) copy-start(s32[1024]{0:T(1024)} %param.7) | copy-start | bytes 12292

commit v4 on v3

--- a/solution.py
+++ b/solution.py
@@ -184,7 +184,7 @@
     local_copy.start()
 
     mic_here = n_split * block
-    body_rows = min(256, mic_here)
+    body_rows = min(512, mic_here)
     nt = (((1,), (1,)), ((), ()))
 
     parts = mic_here // body_rows

time: 46.1 us -> 45.4 us (0.985)
  Pallas kernels: 41.6 us -> 40.8 us
    pallas_call x1, Pallas kernels: 41.6 us -> 40.8 us  [shards(): pl.pallas_call(functools.partial(kernel, cfg), out_shape=jax.ShapeDtypeSt...]
where the time goes in v4:
time: 45.4 us; the launch traced here: 45.1 us
  Pallas kernels  40.8 us (90%)
  local copies, waits for them, and re-layouts  4.28 us (9%)
    pallas_call x1, Pallas kernels, shards(): pl.pallas_call(functools.partial(kernel, cfg), out_shape=jax.ShapeDtypeSt...  40.8 us
    unnamed x9, local copies, waits for them, and re-layouts  4.28 us

profile of v4, /device:TPU:0, one launch (start us, length us, event | category | flops | bytes accessed | tf_op | source)
XLA Modules:
  0.0 45.1 jit_solution(17865151415343828891)
XLA Ops:
  0.0 0.0 copy-start
  0.0 1.2 %copy-done = bf16[2,2,16,8192]{3,2,1,0:T(8,128)(2,1)S(1)} copy-done((bf16[2,2,16,8192]{3,2,1,0:T(8,128)(2,1)S(1)}, bf16[2,2,16,8192]{3,2,1,0:T(8,128)(2,1)}, u32[]{:S(2)}) %copy-start) | copy-done | bytes 1048600
  1.2 0.0 copy-start.1
  1.2 0.9 %copy-done.1 = f32[6,8192]{1,0:T(8,128)S(1)} copy-done((f32[6,8192]{1,0:T(8,128)S(1)}, f32[6,8192]{1,0:T(8,128)}, u32[]{:S(2)}) %copy-start.1) | copy-done | bytes 196632
  2.2 0.0 copy-start.2
  2.2 0.7 %copy-done.2 = f32[3,1024]{1,0:T(4,128)S(1)} copy-done((f32[3,1024]{1,0:T(4,128)S(1)}, f32[3,1024]{1,0:T(4,128)}, u32[]{:S(2)}) %copy-start.2) | copy-done | bytes 12312
  2.9 0.0 copy-start.3
  2.9 0.7 %copy-done.3 = s32[1024]{0:T(1024)S(1)} copy-done((s32[1024]{0:T(1024)S(1)}, s32[1024]{0:T(1024)}, u32[]{:S(2)}) %copy-start.3) | copy-done | bytes 4120
  3.6 40.8 %shard_map.46 = f32[2,128,256]{2,1,0:T(8,128)S(1)} custom-call(bf16[2,2,16,8192]{3,2,1,0:T(8,128)(2,1)S(1)} %copy-done, f32[6,8192]{1,0:T(8,128)S(1)} %copy-done.1, f32[3,1024]{1,0:T(4,128)S(1)} %copy-done.2, s32[1,1024]{1,0:T(1,128)S(1)} %bitcast.1), custom_call_target="tpu_custom_call" | custom-call | flops 2147483648 | bytes 2097152 | tf_op jit(solution)/shard_map/pallas_call | solution.py:375
  44.4 0.7 %copy.6 = f32[2,128,256]{2,1,0:T(8,128)} copy(f32[2,128,256]{2,1,0:T(8,128)S(1)} %shard_map.46) | data formatting | bytes 524288
Async XLA Ops:
  0.0 1.2 %copy-start = (bf16[2,2,16,8192]{3,2,1,0:T(8,128)(2,1)S(1)}, bf16[2,2,16,8192]{3,2,1,0:T(8,128)(2,1)}, u32[]{:S(2)}) copy-start(bf16[2,2,16,8192]{3,2,1,0:T(8,128)(2,1)} %src.1) | copy-start | bytes 3145732
  1.2 0.9 %copy-start.1 = (f32[6,8192]{1,0:T(8,128)S(1)}, f32[6,8192]{1,0:T(8,128)}, u32[]{:S(2)}) copy-start(f32[6,8192]{1,0:T(8,128)} %geom_hbm.1) | copy-start | bytes 589828
  2.2 0.7 %copy-start.2 = (f32[3,1024]{1,0:T(4,128)S(1)}, f32[3,1024]{1,0:T(4,128)}, u32[]{:S(2)}) copy-start(f32[3,1024]{1,0:T(4,128)} %mics_hbm.1) | copy-start | bytes 36868
  2.9 0.7 %copy-start.3 = (s32[1024]{0:T(1024)S(1)}, s32[1024]{0:T(1024)}, u32[]{:S(2)}) copy-start(s32[1024]{0:T(1024)} %param.7) | copy-start | bytes 12292
